TPU v7x, 768 devices: a whole 4x8x12 slice. The times are simulated.
768 devices in a mesh: row: 12 (over z), col: 64 (over y, x, core).
Axes of the slice: x: 4, y: 8, z: 12, core: 2. Of those that a mesh axis runs over, the one named last changes fastest.
Arguments:
- momentum: float32 [6144, 28672], P('row', 'col'), may hold values from -600 to 600
- gradient: bfloat16 [6144, 28672], P('row', 'col'), may hold values from -600 to 600
- right_factor: float32 [28672, 512], P('col'), may hold values from -6 to 6
Outputs:
- momentum_next: float32 [6144, 28672], P('row', 'col')
- right_next: float32 [28672, 512], P('col')
- update: bfloat16 [6144, 28672], P('row', 'col')
All inputs are finite; a program needn't handle non-finite values.
Results may differ from a plain program's by a relative error of at most 0.0015.
Values sent between devices are 32-bit elements; how exact they have to be, the bound alone decides.
No kernel may reach another device: no remote copies, remote signals or barrier semaphores. Data moves between devices by JAX's collectives and lax.ppermute only.
A program may use at most 32 MiB of HBM per device.

v0:
```python
import jax
import jax.numpy as jnp
from jax import lax
from jax.experimental import pallas as pl
from jax.experimental.pallas import tpu as pltpu
from jax.sharding import Mesh, PartitionSpec as P

HIGHEST = lax.Precision.HIGHEST
HIGH = lax.Precision.HIGH
CHIPS = ("y", "x")
TILE = 8
LANES = 128


def dot(a, b, dims, precision=HIGHEST):
    return lax.dot_general(
        a, b, ((dims[:1], dims[1:]), ((), ())), precision=precision, preferred_element_type=jnp.float32
    )


def exchange(blocks, axis):
    return lax.all_to_all(blocks, axis, 0, 0, tiled=True)


def spread(block, axis):
    copies = jnp.broadcast_to(block[None], (lax.axis_size(axis),) + block.shape)
    return exchange(copies, axis).reshape((-1,) + block.shape[1:])


def scatter(whole, axis):
    return jnp.sum(exchange(whole.reshape((lax.axis_size(axis), -1) + whole.shape[1:]), axis), axis=0)


def gather_columns(block):
    return spread(spread(block, CHIPS), "core")


def block_inverse(block):
    shape = (TILE, LANES)
    row = lax.broadcasted_iota(jnp.int32, shape, 0)
    lane = lax.broadcasted_iota(jnp.int32, shape, 1)
    at_row = [row == j for j in range(TILE)]

    def down(x, j):
        return jnp.broadcast_to(x[j : j + 1, :], shape)

    def along(x, k):
        return jnp.broadcast_to(x[:, k : k + 1], shape)

    def combine(columns, rows):
        terms = [c * r for c, r in zip(columns, rows)]
        while len(terms) > 1:
            terms = [terms[i] + terms[i + 1] for i in range(0, len(terms), 2)]
        return terms[0]

    count = LANES // TILE
    strips = [block[TILE * u : TILE * (u + 1), :] for u in range(count)]
    done = []
    for t in range(count):
        first = TILE * t
        inside = (lane >= first) & (lane < first + TILE)
        strip = strips[t]
        columns = [along(strip, first + j) for j in range(TILE)]
        below = [[along(strips[u], first + j) for j in range(TILE)] for u in range(t + 1, count)]
        rows = jnp.where(inside, jnp.where(lane - first == row, 1.0, 0.0), strip)
        rows = [down(rows, j) for j in range(TILE)]
        pivots = jnp.ones(shape, jnp.float32)
        lower = [jnp.where(at_row[m], 1.0, 0.0) for m in range(TILE)]
        for j in range(TILE):
            pivot_row = [down(columns[m], j) for m in range(TILE)]
            inverse = 1.0 / pivot_row[j]
            pivots = jnp.where(at_row[j], pivot_row[j], pivots)
            for m in range(j):
                lower[m] = jnp.where(at_row[j], pivot_row[m], lower[m])
            ratio = columns[j] * inverse
            columns = [
                jnp.where(at_row[j], inverse, -ratio)
                if m == j
                else jnp.where(at_row[j], pivot_row[m] * inverse, columns[m] - ratio * pivot_row[m])
                for m in range(TILE)
            ]
        done.append(jnp.where(lane < first + TILE, combine(lower, rows) * lax.rsqrt(pivots), 0.0))
        solved = combine(columns, rows)
        solved = [down(solved, j) for j in range(TILE)]
        for u in range(t + 1, count):
            strips[u] = jnp.where(inside, 0.0, strips[u]) - combine(below[u - t - 1], solved)
    return jnp.concatenate(done, axis=0)


def inverse_factor_kernel(gram_ref, inverse_ref, work_ref):
    count = gram_ref.shape[0] // LANES
    work_ref[...] = gram_ref[...]
    inverse_ref[...] = jnp.zeros_like(inverse_ref)

    def at(i):
        return slice(LANES * i, LANES * (i + 1))

    for b in range(count):
        inverse = block_inverse(work_ref[at(b), at(b)])
        inverse_ref[at(b), at(b)] = inverse
        before, after = slice(0, LANES * b), slice(LANES * (b + 1), LANES * count)
        if b:
            inverse_ref[at(b), before] = dot(inverse, work_ref[at(b), before], (1, 0))
        if b == count - 1:
            break
        strip = dot(inverse, work_ref[at(b), after], (1, 0))
        for i in range(b + 1, count):
            offset = LANES * (i - b - 1)
            factor = strip[:, offset : offset + LANES]
            rest = slice(LANES * i, LANES * count)
            work_ref[at(i), rest] = work_ref[at(i), rest] - dot(factor, strip[:, offset:], (0, 0))
            work_ref[at(i), at(b)] = -dot(factor, inverse, (0, 0))
            if b:
                work_ref[at(i), before] = work_ref[at(i), before] - dot(
                    factor, inverse_ref[at(b), before], (0, 0)
                )


def inverse_factor(gram):
    return pl.pallas_call(
        inverse_factor_kernel,
        out_shape=jax.ShapeDtypeStruct(gram.shape, jnp.float32),
        in_specs=[pl.BlockSpec(memory_space=pltpu.VMEM)],
        out_specs=pl.BlockSpec(memory_space=pltpu.VMEM),
        scratch_shapes=[pltpu.VMEM(gram.shape, jnp.float32)],
        compiler_params=pltpu.CompilerParams(vmem_limit_bytes=16 * 1024 * 1024),
        cost_estimate=pl.CostEstimate(flops=1 << 30, bytes_accessed=1 << 26, transcendentals=0),
    )(gram)


def correct_kernel(left_ref, inverse_ref, right_ref, momentum_ref, gradient_ref, ortho_ref, next_ref):
    ortho = dot(inverse_ref[...], left_ref[...], (1, 0))
    ortho_ref[...] = ortho
    blend = momentum_ref[...] + gradient_ref[...].astype(jnp.float32)
    next_ref[...] = blend - 0.05 * dot(right_ref[...], ortho, (1, 0))


def correct(left, inverse, right, momentum, gradient):
    vmem = pl.BlockSpec(memory_space=pltpu.VMEM)
    return pl.pallas_call(
        correct_kernel,
        out_shape=(
            jax.ShapeDtypeStruct(left.shape, jnp.float32),
            jax.ShapeDtypeStruct(momentum.shape, jnp.float32),
        ),
        in_specs=[vmem] * 5,
        out_specs=(vmem, vmem),
        compiler_params=pltpu.CompilerParams(vmem_limit_bytes=24 * 1024 * 1024),
        cost_estimate=pl.CostEstimate(flops=1 << 33, bytes_accessed=1 << 23, transcendentals=0),
    )(left, inverse, right, momentum, gradient)


def sum_rows(block):
    share = lax.psum_scatter(block, "row", scatter_dimension=0, tiled=True)
    return lax.all_gather(share, "row", axis=0, tiled=True)


def shards(momentum, gradient, right_factor):
    rank = right_factor.shape[1]
    col = CHIPS + ("core",)
    blend = momentum + gradient.astype(jnp.float32)
    left = gather_columns(scatter(scatter(dot(right_factor, blend, (0, 1)), "core"), CHIPS))
    width = rank // lax.axis_size(col)
    position = lax.axis_index("core") * lax.axis_size(CHIPS) + lax.axis_index(CHIPS)
    mine = lax.dynamic_slice_in_dim(left, position * width, width, 0)
    piece = jnp.sum(spread(dot(mine, left, (1, 1))[None], "row"), axis=0)
    columns = blend.shape[1]
    spare = -columns % (TILE * lax.axis_size("row"))
    crossed = sum_rows(dot(jnp.pad(blend, ((0, 0), (0, spare))), left, (0, 1)))[:columns]
    inverse = inverse_factor(gather_columns(piece))
    right = dot(crossed, inverse, (1, 1))
    squares = jnp.sum(spread(jnp.sum(right * right, axis=0)[None], col), axis=0)
    total_cols = right.shape[0] * lax.axis_size(col)
    total_rows = blend.shape[0] * lax.axis_size("row")
    right_next = right * lax.rsqrt(squares / total_cols + 1e-06)
    ortho, momentum_next = correct(left, inverse, right, momentum.T, gradient.T)
    factor = jnp.sqrt(jnp.float32(total_rows) / rank)
    update = (factor * dot(right_next, ortho, (1, 0), HIGH)).astype(jnp.bfloat16)
    return (momentum_next.T, right_next, update.T)


def solution(mesh):
    rows = mesh.devices.shape[0]
    split = Mesh(mesh.devices.reshape(rows, 8, 4, 2), ("row", "y", "x", "core"))
    col = CHIPS + ("core",)
    return jax.shard_map(
        shards,
        mesh=split,
        in_specs=(P("row", col), P("row", col), P(col, None)),
        out_specs=(P("row", col), P(col, None), P("row", col)),
        check_vma=False,
    )
```

profile of v0, /device:TPU:1, one launch (start us, length us, event | category | flops | bytes accessed | tf_op | source)
XLA Modules:
  0.0 209.8 jit_solution(17560992029530460951)
XLA Ops:
  7.2 0.0 copy-start
  7.2 0.0 reduce-scatter.2.cloned.1.call-start
  7.2 1.5 convert_add_fusion
  8.7 0.0 copy-done
  8.8 1.9 fusion.9
  10.7 14.7 %all_to_all.40 = f32[2,256,512]{2,1,0:T(8,128)S(1)} all-to-all(f32[2,256,512]{2,1,0:T(8,128)S(1)} %bitcast.24), channel_id=1, replica_groups=mesh['row'=12,'y'=8,'x'=4,'core'=2] {'core'}, dimensions={0} | all-to-all | bytes 2097152 | tf_op jit(solution)/shard_map/all_to_all | solution.py:22
  25.4 0.1 reduce_sum.45
  25.5 19.6 %all_to_all.41 = f32[32,8,512]{2,1,0:T(8,128)S(1)} all-to-all(f32[32,8,512]{2,1,0:T(8,128)S(1)} %bitcast.27), channel_id=1, replica_groups=mesh['row'=12,'y'=8,'x'=4,'core'=2] {'y','x'}, dimensions={0} | all-to-all | bytes 1048576 | tf_op jit(solution)/shard_map/all_to_all | solution.py:22
  45.2 0.1 broadcast_in_dim.16
  45.2 20.3 %all_to_all.42 = f32[32,8,512]{2,1,0:T(8,128)S(1)} all-to-all(f32[32,8,512]{2,1,0:T(8,128)S(1)} %broadcast_in_dim.16), channel_id=1, replica_groups=mesh['row'=12,'y'=8,'x'=4,'core'=2] {'y','x'}, dimensions={0} | all-to-all | bytes 1048576 | tf_op jit(solution)/shard_map/all_to_all | solution.py:22
  65.6 0.1 broadcast_in_dim.18
  65.7 7.6 %all_to_all.43 = f32[2,256,512]{2,1,0:T(8,128)S(1)} all-to-all(f32[2,256,512]{2,1,0:T(8,128)S(1)} %broadcast_in_dim.18), channel_id=1, replica_groups=mesh['row'=12,'y'=8,'x'=4,'core'=2] {'core'}, dimensions={0} | all-to-all | bytes 2097152 | tf_op jit(solution)/shard_map/all_to_all | solution.py:22
  73.3 2.8 %fusion.1 = f32[480,512]{1,0:T(8,128)} fusion(f32[512,512]{1,0:T(8,128)S(1)} %bitcast.18, f32[512,448]{0,1:T(8,128)S(1)} %convert_add_fusion), kind=kOutput, calls=%fused_computation.2 | convolution fusion | flops 1509949440 | bytes 2949120 | tf_op jit(solution)/shard_map/dot_general | solution.py:16
  76.0 0.0 reduce-scatter.2.cloned.1.call-update
  76.1 1.0 fusion.5
  77.1 24.5 %all_to_all.44 = f32[12,1,8,512]{3,2,1,0:T(8,128)S(1)} all-to-all(f32[12,1,8,512]{3,2,1,0:T(8,128)S(1)} %broadcast_in_dim.19), channel_id=1, replica_groups=mesh['row'=12,'y'=8,'x'=4,'core'=2] {'row'}, dimensions={0} | all-to-all | bytes 393216 | tf_op jit(solution)/shard_map/all_to_all | solution.py:22
  101.6 0.1 broadcast_in_dim.20
  101.7 17.2 %all_to_all.45 = f32[32,8,512]{2,1,0:T(8,128)S(1)} all-to-all(f32[32,8,512]{2,1,0:T(8,128)S(1)} %broadcast_in_dim.20), channel_id=1, replica_groups=mesh['row'=12,'y'=8,'x'=4,'core'=2] {'y','x'}, dimensions={0} | all-to-all | bytes 1048576 | tf_op jit(solution)/shard_map/all_to_all | solution.py:22
  118.8 0.1 broadcast_in_dim.43
  119.0 10.1 %all_to_all.46 = f32[2,256,512]{2,1,0:T(8,128)S(1)} all-to-all(f32[2,256,512]{2,1,0:T(8,128)S(1)} %broadcast_in_dim.43), channel_id=1, replica_groups=mesh['row'=12,'y'=8,'x'=4,'core'=2] {'core'}, dimensions={0} | all-to-all | bytes 2097152 | tf_op jit(solution)/shard_map/all_to_all | solution.py:22
  129.1 21.6 %shard_map.58.inverse_ref = f32[512,512]{1,0:T(8,128)S(1)} custom-call(f32[512,512]{1,0:T(8,128)S(1)} %bitcast.21), custom_call_target="tpu_custom_call" | custom-call | flops 1073741824 | bytes 67108864 | tf_op jit(solution)/shard_map/pallas_call | solution.py:120
  150.7 0.0 copy-start.3
  150.7 1.0 copy-done.3
  151.7 0.0 reduce-scatter.2.cloned.1.call-done
  151.7 0.0 copy-start.4
  151.7 23.7 %all_gather.3 = f32[480,512]{1,0:T(8,128)S(1)} all-gather(f32[40,512]{1,0:T(8,128)} %reduce-scatter.2.cloned.1.call-done), channel_id=1, replica_groups=mesh['row'=12,'y'=8,'x'=4,'core'=2] {'row'}, dimensions={0}, use_global_device_ids=true | all-gather | bytes 1064960 | tf_op jit(solution)/shard_map/all_gather | solution.py:155
  175.4 0.0 copy-done.4
  175.4 0.0 copy-start.7
  175.4 1.7 multiply_reduce_fusion
  177.1 0.7 broadcast_in_dim.44
  177.8 11.0 %all-to-all-start.7 = ((f32[64,1,512]{2,1,0:T(1,128)}), f32[64,1,512]{2,1,0:T(1,128)S(1)}, u32[]{:S(2)}, u32[]{:S(2)}) async-start(f32[64,1,512]{2,1,0:T(1,128)} %broadcast_in_dim.44), calls=%async_computation.8 | async-start | bytes 262144 | tf_op jit(solution)/shard_map/all_to_all | solution.py:22
  188.8 0.0 copy-done.7
  188.8 0.0 copy-start.5
  188.8 1.2 copy-done.5
  190.0 0.0 copy-start.6
  190.0 1.2 copy-done.6
  191.2 4.4 %shard_map.59 = (f32[512,512]{1,0:T(8,128)S(1)}, f32[448,512]{1,0:T(8,128)}) custom-call(f32[512,512]{1,0:T(8,128)S(1)} %bitcast.20, f32[512,512]{1,0:T(8,128)S(1)} %copy-done.5, f32[448,512]{1,0:T(8,128)S(1)} %get-tuple-element.8.right_ref, f32[448,512]{1,0:T(8,128)S(1)} %bitcast.22, bf16[448,512]{1,0:T(8,128)(2,1)S(1)} %bitcast.23), custom_call_target="tpu_custom_call" | custom-call | flops 8589934592 | bytes 8388608 | tf_op jit(solution)/shard_map/pallas_call | solution.py:140
  195.6 0.0 copy-start.1
  195.6 1.0 copy-done.1
  196.6 3.4 %all-to-all-done.7 = f32[64,1,512]{2,1,0:T(1,128)S(1)} async-done(((f32[64,1,512]{2,1,0:T(1,128)}), f32[64,1,512]{2,1,0:T(1,128)S(1)}, u32[]{:S(2)}, u32[]{:S(2)}) %all-to-all-start.7) | async-done | bytes 131104 | tf_op jit(solution)/shard_map/all_to_all | solution.py:22
  199.9 0.0 copy-start.2
  199.9 0.1 reduce_sum.49
  200.0 0.1 broadcast_multiply_fusion
  200.2 0.0 copy-start.8
  200.2 1.1 copy-done.2
  201.2 1.7 fusion
  202.9 0.0 copy-done.8
  (4 shorter events, 0.1 us)
Async XLA Ops:
  7.2 1.6 copy-start
  7.2 144.5 %reduce-scatter.2.cloned.1.call-start = ((), (), s32[]{:S(2)}) async-start(), calls=%async_computation.9 | async-start | bytes 1064960 | tf_op jit(solution)/shard_map/reduce_scatter | solution.py:154
  150.7 1.0 copy-start.3
  151.7 23.7 %copy-start.4 = (f32[512,512]{1,0:T(8,128)S(1)}, f32[512,512]{1,0:T(8,128)}, u32[]{:S(2)}) copy-start(f32[512,512]{1,0:T(8,128)} %copy-done.3) | copy-start | bytes 3145732
  175.4 13.4 %copy-start.7 = (bf16[512,448]{0,1:T(8,128)(2,1)S(1)}, bf16[512,448]{0,1:T(8,128)(2,1)}, u32[]{:S(2)}) copy-start(bf16[512,448]{0,1:T(8,128)(2,1)} %param.4) | copy-start | bytes 1376260
  177.8 22.1 %all-to-all-start.7 = ((f32[64,1,512]{2,1,0:T(1,128)}), f32[64,1,512]{2,1,0:T(1,128)S(1)}, u32[]{:S(2)}, u32[]{:S(2)}) async-start(f32[64,1,512]{2,1,0:T(1,128)} %broadcast_in_dim.44), calls=%async_computation.8 | async-start | bytes 262144 | tf_op jit(solution)/shard_map/all_to_all | solution.py:22
  188.8 1.2 copy-start.5
  190.0 1.2 copy-start.6
  195.6 1.0 copy-start.1
  199.9 1.3 copy-start.2
  200.2 2.7 %copy-start.8 = (f32[448,512]{1,0:T(8,128)}, f32[448,512]{1,0:T(8,128)S(1)}, u32[]{:S(2)}) copy-start(f32[448,512]{1,0:T(8,128)S(1)} %broadcast_multiply_fusion) | copy-start | bytes 2752516
Sparse Core Ops, SparseCore 0:
  76.2 51.8 reduce-scatter.1
where the time goes:
time: 210 us
  blocking collectives  138 us (66%)
  Pallas kernels  25.9 us (12%)
  between operations  14.2 us (7%)
  starting transfers between devices  11 us (5%)
  matrix products  8.95 us (4%)
  local copies, waits for them, and re-layouts  6.57 us (3%)
  waiting for transfers between devices  3.37 us (2%)
    all_to_all x7, blocking collectives, exchange(): return lax.all_to_all(blocks, axis, 0, 0, tiled=True)  114 us
    all_gather x1, blocking collectives, sum_rows(): return lax.all_gather(share, 'row', axis=0, tiled=True)  23.7 us
    pallas_call x1, Pallas kernels, inverse_factor(): pl.pallas_call(inverse_factor_kernel, out_shape=jax.ShapeDtypeStruct(gram...  21.6 us
    all_to_all x1, starting transfers between devices, exchange(): return lax.all_to_all(blocks, axis, 0, 0, tiled=True)  11 us
    dot_general x5, matrix products, dot(): lax.dot_general(a, b, ((dims[:1], dims[1:]), ((), ())), precision=precisi...  8.95 us
    unnamed x18, local copies, waits for them, and re-layouts  5.47 us
    pallas_call x1, Pallas kernels, correct(): pl.pallas_call(correct_kernel, out_shape=(jax.ShapeDtypeStruct(left.shape...  4.36 us
  transfers between devices with their start and end apart: 2, of which 1 were waited for; matrix products, arithmetic and copies ran while one was open for 1% of the time, Pallas kernels for 12%

commit v1 on v0

--- a/solution.py
+++ b/solution.py
@@ -1,3 +1,5 @@
+import functools
+
 import jax
 import jax.numpy as jnp
 from jax import lax
@@ -35,7 +37,7 @@
     return spread(spread(block, CHIPS), "core")
 
 
-def block_inverse(block):
+def block_inverse(block, later):
     shape = (TILE, LANES)
     row = lax.broadcasted_iota(jnp.int32, shape, 0)
     lane = lax.broadcasted_iota(jnp.int32, shape, 1)
@@ -53,6 +55,7 @@
             terms = [terms[i] + terms[i + 1] for i in range(0, len(terms), 2)]
         return terms[0]
 
+    later = list(later)
     count = LANES // TILE
     strips = [block[TILE * u : TILE * (u + 1), :] for u in range(count)]
     done = []
@@ -61,59 +64,103 @@
         inside = (lane >= first) & (lane < first + TILE)
         strip = strips[t]
         columns = [along(strip, first + j) for j in range(TILE)]
-        below = [[along(strips[u], first + j) for j in range(TILE)] for u in range(t + 1, count)]
         rows = jnp.where(inside, jnp.where(lane - first == row, 1.0, 0.0), strip)
         rows = [down(rows, j) for j in range(TILE)]
         pivots = jnp.ones(shape, jnp.float32)
         lower = [jnp.where(at_row[m], 1.0, 0.0) for m in range(TILE)]
-        for j in range(TILE):
-            pivot_row = [down(columns[m], j) for m in range(TILE)]
-            inverse = 1.0 / pivot_row[j]
-            pivots = jnp.where(at_row[j], pivot_row[j], pivots)
+        for j in range(0, TILE, 2):
+            k = j + 1
+            upper_row = [down(columns[m], j) for m in range(TILE)]
+            lower_row = [down(columns[m], k) for m in range(TILE)]
+            a, b, d = upper_row[j], lower_row[j], lower_row[k]
+            scale = 1.0 / (a * d - b * b)
+            at_j = jnp.where(at_row[j], -1.0, jnp.where(at_row[k], 0.0, columns[j]))
+            at_k = jnp.where(at_row[k], -1.0, jnp.where(at_row[j], 0.0, columns[k]))
+            ratio_j = (at_j * d - at_k * b) * scale
+            ratio_k = (at_k * a - at_j * b) * scale
+            step = b / a
+            pivots = jnp.where(at_row[j], a, jnp.where(at_row[k], d - b * step, pivots))
             for m in range(j):
-                lower[m] = jnp.where(at_row[j], pivot_row[m], lower[m])
-            ratio = columns[j] * inverse
+                lower[m] = jnp.where(
+                    at_row[j], upper_row[m], jnp.where(at_row[k], lower_row[m] - step * upper_row[m], lower[m])
+                )
+            lower[j] = jnp.where(at_row[k], -step, lower[j])
+            pair = at_row[j] | at_row[k]
             columns = [
-                jnp.where(at_row[j], inverse, -ratio)
+                -ratio_j
                 if m == j
-                else jnp.where(at_row[j], pivot_row[m] * inverse, columns[m] - ratio * pivot_row[m])
+                else -ratio_k
+                if m == k
+                else (jnp.where(pair, 0.0, columns[m]) - ratio_j * upper_row[m]) - ratio_k * lower_row[m]
                 for m in range(TILE)
             ]
         done.append(jnp.where(lane < first + TILE, combine(lower, rows) * lax.rsqrt(pivots), 0.0))
         solved = combine(columns, rows)
         solved = [down(solved, j) for j in range(TILE)]
         for u in range(t + 1, count):
-            strips[u] = jnp.where(inside, 0.0, strips[u]) - combine(below[u - t - 1], solved)
+            below = [along(strips[u], first + j) for j in range(TILE)]
+            strips[u] = jnp.where(inside, 0.0, strips[u]) - combine(below, solved)
+        if later:
+            later.pop(0)()
+    for call in later:
+        call()
     return jnp.concatenate(done, axis=0)
 
 
 def inverse_factor_kernel(gram_ref, inverse_ref, work_ref):
     count = gram_ref.shape[0] // LANES
-    work_ref[...] = gram_ref[...]
-    inverse_ref[...] = jnp.zeros_like(inverse_ref)
 
     def at(i):
         return slice(LANES * i, LANES * (i + 1))
 
+    square = (LANES, LANES)
+    eye = lax.broadcasted_iota(jnp.int32, square, 0) == lax.broadcasted_iota(jnp.int32, square, 1)
+    diagonal = [jnp.where(eye, gram_ref[at(i), at(i)], 0.0) for i in range(count)]
+    by_lane = [lax.rsqrt(jnp.sum(d, axis=0, keepdims=True)) for d in diagonal]
+    by_row = [lax.rsqrt(jnp.sum(d, axis=1, keepdims=True)) for d in diagonal]
+    for i in range(count):
+        for j in range(i, count):
+            work_ref[at(i), at(j)] = gram_ref[at(i), at(j)] * by_row[i] * by_lane[j]
+    inverse_ref[...] = jnp.zeros_like(inverse_ref)
+
+    later = []
     for b in range(count):
-        inverse = block_inverse(work_ref[at(b), at(b)])
+        inverse = block_inverse(work_ref[at(b), at(b)], later)
         inverse_ref[at(b), at(b)] = inverse
-        before, after = slice(0, LANES * b), slice(LANES * (b + 1), LANES * count)
-        if b:
+        before = slice(0, LANES * b)
+        factor = {}
+
+        def finish(b=b, before=before, inverse=inverse):
             inverse_ref[at(b), before] = dot(inverse, work_ref[at(b), before], (1, 0))
+
+        def strip(i, b=b, inverse=inverse, factor=factor):
+            factor[i] = dot(inverse, work_ref[at(b), at(i)], (1, 0))
+
+        def update(i, j, factor=factor):
+            work_ref[at(i), at(j)] = work_ref[at(i), at(j)] - dot(factor[i], factor[j], (0, 0))
+
+        def carry(i, b=b, inverse=inverse, factor=factor):
+            work_ref[at(i), at(b)] = -dot(factor[i], inverse, (0, 0))
+
+        def carry_before(i, b=b, before=before, factor=factor):
+            work_ref[at(i), before] = work_ref[at(i), before] - dot(factor[i], inverse_ref[at(b), before], (0, 0))
+
+        later = [finish] if b else []
         if b == count - 1:
             break
-        strip = dot(inverse, work_ref[at(b), after], (1, 0))
+        strip(b + 1)
+        update(b + 1, b + 1)
+        later += [functools.partial(strip, i) for i in range(b + 2, count)]
         for i in range(b + 1, count):
-            offset = LANES * (i - b - 1)
-            factor = strip[:, offset : offset + LANES]
-            rest = slice(LANES * i, LANES * count)
-            work_ref[at(i), rest] = work_ref[at(i), rest] - dot(factor, strip[:, offset:], (0, 0))
-            work_ref[at(i), at(b)] = -dot(factor, inverse, (0, 0))
+            later += [functools.partial(update, i, j) for j in range(i, count) if (i, j) != (b + 1, b + 1)]
+            later.append(functools.partial(carry, i))
             if b:
-                work_ref[at(i), before] = work_ref[at(i), before] - dot(
-                    factor, inverse_ref[at(b), before], (0, 0)
-                )
+                later.append(functools.partial(carry_before, i))
+    for call in later:
+        call()
+    for i in range(count):
+        for j in range(i + 1):
+            inverse_ref[at(i), at(j)] = inverse_ref[at(i), at(j)] * by_lane[j]
 
 
 def inverse_factor(gram):

time: 210 us -> 207 us (0.986)
  Pallas kernels: 25.9 us -> 22.4 us
    pallas_call x1, Pallas kernels: 21.6 us -> 18 us  [inverse_factor(): pl.pallas_call(inverse_factor_kernel, out_shape=jax.ShapeDtypeStruct(gram...]
  transfers between devices with their start and end apart: 2 -> 2, of which waited for: 1 -> 1; matrix products, arithmetic and copies ran while one was open for 1% -> 1% of each run, Pallas kernels for 12% -> 11%
where the time goes in v1:
time: 207 us; the launch traced here: 206 us
  blocking collectives  138 us (67%)
  Pallas kernels  22.4 us (11%)
  between operations  14.2 us (7%)
  starting transfers between devices  11 us (5%)
  matrix products  8.95 us (4%)
  local copies, waits for them, and re-layouts  6.57 us (3%)
  waiting for transfers between devices  3.37 us (2%)
    all_to_all x7, blocking collectives, exchange(): return lax.all_to_all(blocks, axis, 0, 0, tiled=True)  114 us
    all_gather x1, blocking collectives, sum_rows(): return lax.all_gather(share, 'row', axis=0, tiled=True)  23.7 us
    pallas_call x1, Pallas kernels, inverse_factor(): pl.pallas_call(inverse_factor_kernel, out_shape=jax.ShapeDtypeStruct(gram...  18 us
    all_to_all x1, starting transfers between devices, exchange(): return lax.all_to_all(blocks, axis, 0, 0, tiled=True)  11 us
    dot_general x5, matrix products, dot(): lax.dot_general(a, b, ((dims[:1], dims[1:]), ((), ())), precision=precisi...  8.95 us
    unnamed x18, local copies, waits for them, and re-layouts  5.47 us
    pallas_call x1, Pallas kernels, correct(): pl.pallas_call(correct_kernel, out_shape=(jax.ShapeDtypeStruct(left.shape...  4.36 us
  transfers between devices with their start and end apart: 2, of which 1 were waited for; matrix products, arithmetic and copies ran while one was open for 1% of the time, Pallas kernels for 11%

profile of v1, /device:TPU:1, one launch (start us, length us, event | category | flops | bytes accessed | tf_op | source)
XLA Modules:
  0.0 206.2 jit_solution(15572220653539355669)
XLA Ops:
  7.2 0.0 copy-start
  7.2 0.0 reduce-scatter.2.cloned.1.call-start
  7.2 1.5 convert_add_fusion
  8.7 0.0 copy-done
  8.8 1.9 fusion.9
  10.7 14.7 %all_to_all.40 = f32[2,256,512]{2,1,0:T(8,128)S(1)} all-to-all(f32[2,256,512]{2,1,0:T(8,128)S(1)} %bitcast.24), channel_id=1, replica_groups=mesh['row'=12,'y'=8,'x'=4,'core'=2] {'core'}, dimensions={0} | all-to-all | bytes 2097152 | tf_op jit(solution)/shard_map/all_to_all | solution.py:24
  25.4 0.1 reduce_sum.45
  25.5 19.6 %all_to_all.41 = f32[32,8,512]{2,1,0:T(8,128)S(1)} all-to-all(f32[32,8,512]{2,1,0:T(8,128)S(1)} %bitcast.27), channel_id=1, replica_groups=mesh['row'=12,'y'=8,'x'=4,'core'=2] {'y','x'}, dimensions={0} | all-to-all | bytes 1048576 | tf_op jit(solution)/shard_map/all_to_all | solution.py:24
  45.2 0.1 broadcast_in_dim.16
  45.2 20.3 %all_to_all.42 = f32[32,8,512]{2,1,0:T(8,128)S(1)} all-to-all(f32[32,8,512]{2,1,0:T(8,128)S(1)} %broadcast_in_dim.16), channel_id=1, replica_groups=mesh['row'=12,'y'=8,'x'=4,'core'=2] {'y','x'}, dimensions={0} | all-to-all | bytes 1048576 | tf_op jit(solution)/shard_map/all_to_all | solution.py:24
  65.6 0.1 broadcast_in_dim.18
  65.7 7.6 %all_to_all.43 = f32[2,256,512]{2,1,0:T(8,128)S(1)} all-to-all(f32[2,256,512]{2,1,0:T(8,128)S(1)} %broadcast_in_dim.18), channel_id=1, replica_groups=mesh['row'=12,'y'=8,'x'=4,'core'=2] {'core'}, dimensions={0} | all-to-all | bytes 2097152 | tf_op jit(solution)/shard_map/all_to_all | solution.py:24
  73.3 2.8 %fusion.1 = f32[480,512]{1,0:T(8,128)} fusion(f32[512,512]{1,0:T(8,128)S(1)} %bitcast.18, f32[512,448]{0,1:T(8,128)S(1)} %convert_add_fusion), kind=kOutput, calls=%fused_computation.2 | convolution fusion | flops 1509949440 | bytes 2949120 | tf_op jit(solution)/shard_map/dot_general | solution.py:18
  76.0 0.0 reduce-scatter.2.cloned.1.call-update
  76.1 1.0 fusion.5
  77.1 24.5 %all_to_all.44 = f32[12,1,8,512]{3,2,1,0:T(8,128)S(1)} all-to-all(f32[12,1,8,512]{3,2,1,0:T(8,128)S(1)} %broadcast_in_dim.19), channel_id=1, replica_groups=mesh['row'=12,'y'=8,'x'=4,'core'=2] {'row'}, dimensions={0} | all-to-all | bytes 393216 | tf_op jit(solution)/shard_map/all_to_all | solution.py:24
  101.6 0.1 broadcast_in_dim.20
  101.7 17.2 %all_to_all.45 = f32[32,8,512]{2,1,0:T(8,128)S(1)} all-to-all(f32[32,8,512]{2,1,0:T(8,128)S(1)} %broadcast_in_dim.20), channel_id=1, replica_groups=mesh['row'=12,'y'=8,'x'=4,'core'=2] {'y','x'}, dimensions={0} | all-to-all | bytes 1048576 | tf_op jit(solution)/shard_map/all_to_all | solution.py:24
  118.8 0.1 broadcast_in_dim.43
  119.0 10.1 %all_to_all.46 = f32[2,256,512]{2,1,0:T(8,128)S(1)} all-to-all(f32[2,256,512]{2,1,0:T(8,128)S(1)} %broadcast_in_dim.43), channel_id=1, replica_groups=mesh['row'=12,'y'=8,'x'=4,'core'=2] {'core'}, dimensions={0} | all-to-all | bytes 2097152 | tf_op jit(solution)/shard_map/all_to_all | solution.py:24
  129.1 18.0 %shard_map.58.inverse_ref = f32[512,512]{1,0:T(8,128)S(1)} custom-call(f32[512,512]{1,0:T(8,128)S(1)} %bitcast.21), custom_call_target="tpu_custom_call" | custom-call | flops 1073741824 | bytes 67108864 | tf_op jit(solution)/shard_map/pallas_call | solution.py:167
  147.1 0.0 copy-start.3
  147.2 1.0 copy-done.3
  148.1 0.0 reduce-scatter.2.cloned.1.call-done
  148.1 0.0 copy-start.4
  148.1 23.7 %all_gather.3 = f32[480,512]{1,0:T(8,128)S(1)} all-gather(f32[40,512]{1,0:T(8,128)} %reduce-scatter.2.cloned.1.call-done), channel_id=1, replica_groups=mesh['row'=12,'y'=8,'x'=4,'core'=2] {'row'}, dimensions={0}, use_global_device_ids=true | all-gather | bytes 1064960 | tf_op jit(solution)/shard_map/all_gather | solution.py:202
  171.8 0.0 copy-done.4
  171.8 0.0 copy-start.7
  171.8 1.7 multiply_reduce_fusion
  173.5 0.7 broadcast_in_dim.44
  174.3 11.0 %all-to-all-start.7 = ((f32[64,1,512]{2,1,0:T(1,128)}), f32[64,1,512]{2,1,0:T(1,128)S(1)}, u32[]{:S(2)}, u32[]{:S(2)}) async-start(f32[64,1,512]{2,1,0:T(1,128)} %broadcast_in_dim.44), calls=%async_computation.8 | async-start | bytes 262144 | tf_op jit(solution)/shard_map/all_to_all | solution.py:24
  185.3 0.0 copy-done.7
  185.3 0.0 copy-start.5
  185.3 1.2 copy-done.5
  186.5 0.0 copy-start.6
  186.5 1.2 copy-done.6
  187.7 4.4 %shard_map.59 = (f32[512,512]{1,0:T(8,128)S(1)}, f32[448,512]{1,0:T(8,128)}) custom-call(f32[512,512]{1,0:T(8,128)S(1)} %bitcast.20, f32[512,512]{1,0:T(8,128)S(1)} %copy-done.5, f32[448,512]{1,0:T(8,128)S(1)} %get-tuple-element.8.right_ref, f32[448,512]{1,0:T(8,128)S(1)} %bitcast.22, bf16[448,512]{1,0:T(8,128)(2,1)S(1)} %bitcast.23), custom_call_target="tpu_custom_call" | custom-call | flops 8589934592 | bytes 8388608 | tf_op jit(solution)/shard_map/pallas_call | solution.py:187
  192.0 0.0 copy-start.1
  192.0 1.0 copy-done.1
  193.0 3.4 %all-to-all-done.7 = f32[64,1,512]{2,1,0:T(1,128)S(1)} async-done(((f32[64,1,512]{2,1,0:T(1,128)}), f32[64,1,512]{2,1,0:T(1,128)S(1)}, u32[]{:S(2)}, u32[]{:S(2)}) %all-to-all-start.7) | async-done | bytes 131104 | tf_op jit(solution)/shard_map/all_to_all | solution.py:24
  196.4 0.0 copy-start.2
  196.4 0.1 reduce_sum.49
  196.5 0.1 broadcast_multiply_fusion
  196.6 0.0 copy-start.8
  196.7 1.1 copy-done.2
  197.7 1.7 fusion
  199.4 0.0 copy-done.8
  (4 shorter events, 0.1 us)
Async XLA Ops:
  7.2 1.6 copy-start
  7.2 141.0 %reduce-scatter.2.cloned.1.call-start = ((), (), s32[]{:S(2)}) async-start(), calls=%async_computation.9 | async-start | bytes 1064960 | tf_op jit(solution)/shard_map/reduce_scatter | solution.py:201
  147.1 1.0 copy-start.3
  148.1 23.7 %copy-start.4 = (f32[512,512]{1,0:T(8,128)S(1)}, f32[512,512]{1,0:T(8,128)}, u32[]{:S(2)}) copy-start(f32[512,512]{1,0:T(8,128)} %copy-done.3) | copy-start | bytes 3145732
  171.8 13.4 %copy-start.7 = (bf16[512,448]{0,1:T(8,128)(2,1)S(1)}, bf16[512,448]{0,1:T(8,128)(2,1)}, u32[]{:S(2)}) copy-start(bf16[512,448]{0,1:T(8,128)(2,1)} %param.4) | copy-start | bytes 1376260
  174.3 22.1 %all-to-all-start.7 = ((f32[64,1,512]{2,1,0:T(1,128)}), f32[64,1,512]{2,1,0:T(1,128)S(1)}, u32[]{:S(2)}, u32[]{:S(2)}) async-start(f32[64,1,512]{2,1,0:T(1,128)} %broadcast_in_dim.44), calls=%async_computation.8 | async-start | bytes 262144 | tf_op jit(solution)/shard_map/all_to_all | solution.py:24
  185.3 1.2 copy-start.5
  186.5 1.2 copy-start.6
  192.0 1.0 copy-start.1
  196.4 1.3 copy-start.2
  196.6 2.7 %copy-start.8 = (f32[448,512]{1,0:T(8,128)}, f32[448,512]{1,0:T(8,128)S(1)}, u32[]{:S(2)}) copy-start(f32[448,512]{1,0:T(8,128)S(1)} %broadcast_multiply_fusion) | copy-start | bytes 2752516
Sparse Core Ops, SparseCore 0:
  76.2 51.8 reduce-scatter.1

commit v2 on v1

--- a/solution.py
+++ b/solution.py
@@ -113,14 +113,18 @@
     def at(i):
         return slice(LANES * i, LANES * (i + 1))
 
+    def gram(i, j):
+        row, slot = (i, j - i) if j - i < count - 1 else (count // 2, count - 2)
+        return gram_ref[at(row), at(slot)]
+
     square = (LANES, LANES)
     eye = lax.broadcasted_iota(jnp.int32, square, 0) == lax.broadcasted_iota(jnp.int32, square, 1)
-    diagonal = [jnp.where(eye, gram_ref[at(i), at(i)], 0.0) for i in range(count)]
+    diagonal = [jnp.where(eye, gram(i, i), 0.0) for i in range(count)]
     by_lane = [lax.rsqrt(jnp.sum(d, axis=0, keepdims=True)) for d in diagonal]
     by_row = [lax.rsqrt(jnp.sum(d, axis=1, keepdims=True)) for d in diagonal]
     for i in range(count):
         for j in range(i, count):
-            work_ref[at(i), at(j)] = gram_ref[at(i), at(j)] * by_row[i] * by_lane[j]
+            work_ref[at(i), at(j)] = gram(i, j) * by_row[i] * by_lane[j]
     inverse_ref[...] = jnp.zeros_like(inverse_ref)
 
     later = []
@@ -163,16 +167,36 @@
             inverse_ref[at(i), at(j)] = inverse_ref[at(i), at(j)] * by_lane[j]
 
 
-def inverse_factor(gram):
+def inverse_factor(packed):
+    square = (packed.shape[0], packed.shape[0])
     return pl.pallas_call(
         inverse_factor_kernel,
-        out_shape=jax.ShapeDtypeStruct(gram.shape, jnp.float32),
+        out_shape=jax.ShapeDtypeStruct(square, jnp.float32),
         in_specs=[pl.BlockSpec(memory_space=pltpu.VMEM)],
         out_specs=pl.BlockSpec(memory_space=pltpu.VMEM),
-        scratch_shapes=[pltpu.VMEM(gram.shape, jnp.float32)],
+        scratch_shapes=[pltpu.VMEM(square, jnp.float32)],
         compiler_params=pltpu.CompilerParams(vmem_limit_bytes=16 * 1024 * 1024),
         cost_estimate=pl.CostEstimate(flops=1 << 30, bytes_accessed=1 << 26, transcendentals=0),
-    )(gram)
+    )(packed)
+
+
+def pack_strip(left, position):
+    count = left.shape[0] // LANES
+    strips = LANES // TILE
+    level = position // strips
+    other = position - strips * (count // 2)
+    mine = lax.dynamic_slice_in_dim(left, position * TILE, TILE, 0)
+    borrowed = lax.dynamic_slice_in_dim(left, jnp.maximum(other, 0) * TILE, TILE, 0)
+    product = dot(jnp.concatenate([mine, borrowed], axis=0), left, (1, 1))
+    blocks = [product[:TILE, LANES * j : LANES * (j + 1)] for j in range(count)]
+    slots = []
+    for slot in range(count - 1):
+        choice = blocks[count - 1]
+        for i in range(count - 1 - slot):
+            choice = jnp.where(level == i, blocks[i + slot], choice)
+        slots.append(choice)
+    slots[-1] = jnp.where(level == count // 2, product[TILE:, LANES * (count - 1) :], slots[-1])
+    return jnp.concatenate(slots, axis=1)
 
 
 def correct_kernel(left_ref, inverse_ref, right_ref, momentum_ref, gradient_ref, ortho_ref, next_ref):
@@ -207,10 +231,8 @@
     col = CHIPS + ("core",)
     blend = momentum + gradient.astype(jnp.float32)
     left = gather_columns(scatter(scatter(dot(right_factor, blend, (0, 1)), "core"), CHIPS))
-    width = rank // lax.axis_size(col)
     position = lax.axis_index("core") * lax.axis_size(CHIPS) + lax.axis_index(CHIPS)
-    mine = lax.dynamic_slice_in_dim(left, position * width, width, 0)
-    piece = jnp.sum(spread(dot(mine, left, (1, 1))[None], "row"), axis=0)
+    piece = jnp.sum(spread(pack_strip(left, position)[None], "row"), axis=0)
     columns = blend.shape[1]
     spare = -columns % (TILE * lax.axis_size("row"))
     crossed = sum_rows(dot(jnp.pad(blend, ((0, 0), (0, spare))), left, (0, 1)))[:columns]

time: 207 us -> 203 us (0.981)
  blocking collectives: 138 us -> 113 us
  waiting for transfers between devices: 3.37 us -> 18.7 us
  starting transfers between devices: 11 us -> 15.1 us
    all_to_all x7 -> x6, blocking collectives: 114 us -> 90.1 us  [exchange(): return lax.all_to_all(blocks, axis, 0, 0, tiled=True)]
    all_to_all x1 -> x2, waiting for transfers between devices: 3.35 us -> 18.7 us  [exchange(): return lax.all_to_all(blocks, axis, 0, 0, tiled=True)]
    all_to_all x1 -> x2, starting transfers between devices: 11 us -> 15.1 us  [exchange(): return lax.all_to_all(blocks, axis, 0, 0, tiled=True)]
  transfers between devices with their start and end apart: 2 -> 3, of which waited for: 1 -> 2; matrix products, arithmetic and copies ran while one was open for 1% -> 1% of each run, Pallas kernels for 11% -> 11%
where the time goes in v2:
time: 203 us; the launch traced here: 202 us
  blocking collectives  113 us (56%)
  Pallas kernels  22.4 us (11%)
  waiting for transfers between devices  18.7 us (9%)
  starting transfers between devices  15.1 us (7%)
  between operations  14.2 us (7%)
  matrix products  8.97 us (4%)
  local copies, waits for them, and re-layouts  7.28 us (4%)
    all_to_all x6, blocking collectives, exchange(): return lax.all_to_all(blocks, axis, 0, 0, tiled=True)  90.1 us
    all_gather x1, blocking collectives, sum_rows(): return lax.all_gather(share, 'row', axis=0, tiled=True)  23.4 us
    all_to_all x2, waiting for transfers between devices, exchange(): return lax.all_to_all(blocks, axis, 0, 0, tiled=True)  18.7 us
    pallas_call x1, Pallas kernels, inverse_factor(): pl.pallas_call(inverse_factor_kernel, out_shape=jax.ShapeDtypeStruct(squa...  18 us
    all_to_all x2, starting transfers between devices, exchange(): return lax.all_to_all(blocks, axis, 0, 0, tiled=True)  15.1 us
    dot_general x5, matrix products, dot(): lax.dot_general(a, b, ((dims[:1], dims[1:]), ((), ())), precision=precisi...  8.97 us
    unnamed x18, local copies, waits for them, and re-layouts  5.47 us
    pallas_call x1, Pallas kernels, correct(): pl.pallas_call(correct_kernel, out_shape=(jax.ShapeDtypeStruct(left.shape...  4.36 us
  transfers between devices with their start and end apart: 3, of which 2 were waited for; matrix products, arithmetic and copies ran while one was open for 1% of the time, Pallas kernels for 11%

profile of v2, /device:TPU:1, one launch (start us, length us, event | category | flops | bytes accessed | tf_op | source)
XLA Modules:
  0.0 202.1 jit_solution(11388359210245964068)
XLA Ops:
  7.2 0.0 copy-start
  7.2 1.5 convert_add_fusion
  8.7 0.1 copy-done
  8.8 1.9 fusion.13
  10.7 14.7 %all_to_all.40 = f32[2,256,512]{2,1,0:T(8,128)S(1)} all-to-all(f32[2,256,512]{2,1,0:T(8,128)S(1)} %bitcast.25), channel_id=1, replica_groups=mesh['row'=12,'y'=8,'x'=4,'core'=2] {'core'}, dimensions={0} | all-to-all | bytes 2097152 | tf_op jit(solution)/shard_map/all_to_all | solution.py:24
  25.4 0.1 reduce_sum.45
  25.5 19.6 %all_to_all.41 = f32[32,8,512]{2,1,0:T(8,128)S(1)} all-to-all(f32[32,8,512]{2,1,0:T(8,128)S(1)} %bitcast.27), channel_id=1, replica_groups=mesh['row'=12,'y'=8,'x'=4,'core'=2] {'y','x'}, dimensions={0} | all-to-all | bytes 1048576 | tf_op jit(solution)/shard_map/all_to_all | solution.py:24
  45.2 0.9 broadcast_in_dim.16
  46.0 5.1 %all-to-all-start.2 = ((f32[32,8,512]{2,1,0:T(8,128)}), f32[32,8,512]{2,1,0:T(8,128)S(1)}, u32[]{:S(2)}, u32[]{:S(2)}) async-start(f32[32,8,512]{2,1,0:T(8,128)} %broadcast_in_dim.16), calls=%async_computation.2 | async-start | bytes 1048576 | tf_op jit(solution)/shard_map/all_to_all | solution.py:24
  51.1 0.0 reduce-scatter.2.cloned.1.call-start
  51.2 15.3 %all-to-all-done.2 = f32[32,8,512]{2,1,0:T(8,128)S(1)} async-done(((f32[32,8,512]{2,1,0:T(8,128)}), f32[32,8,512]{2,1,0:T(8,128)S(1)}, u32[]{:S(2)}, u32[]{:S(2)}) %all-to-all-start.2) | async-done | bytes 524320 | tf_op jit(solution)/shard_map/all_to_all | solution.py:24
  66.6 0.1 broadcast_in_dim.18
  66.7 7.6 %all_to_all.42 = f32[2,256,512]{2,1,0:T(8,128)S(1)} all-to-all(f32[2,256,512]{2,1,0:T(8,128)S(1)} %broadcast_in_dim.18), channel_id=1, replica_groups=mesh['row'=12,'y'=8,'x'=4,'core'=2] {'core'}, dimensions={0} | all-to-all | bytes 2097152 | tf_op jit(solution)/shard_map/all_to_all | solution.py:24
  74.3 2.8 %fusion.1 = f32[480,512]{1,0:T(8,128)} fusion(f32[512,512]{1,0:T(8,128)S(1)} %bitcast.18, f32[512,448]{0,1:T(8,128)S(1)} %convert_add_fusion), kind=kOutput, calls=%fused_computation.2 | convolution fusion | flops 1509949440 | bytes 2949120 | tf_op jit(solution)/shard_map/dot_general | solution.py:18
  77.1 0.0 reduce-scatter.2.cloned.1.call-update
  77.1 1.0 fusion.5
  78.1 23.5 %all_to_all.43 = f32[12,1,8,384]{3,2,1,0:T(8,128)S(1)} all-to-all(f32[12,1,8,384]{3,2,1,0:T(8,128)S(1)} %broadcast_in_dim.19), channel_id=1, replica_groups=mesh['row'=12,'y'=8,'x'=4,'core'=2] {'row'}, dimensions={0} | all-to-all | bytes 294912 | tf_op jit(solution)/shard_map/all_to_all | solution.py:24
  101.7 15.4 %all_to_all.44 = f32[32,8,384]{2,1,0:T(8,128)S(1)} all-to-all(f32[32,8,384]{2,1,0:T(8,128)S(1)} %broadcast_in_dim.20), channel_id=1, replica_groups=mesh['row'=12,'y'=8,'x'=4,'core'=2] {'y','x'}, dimensions={0} | all-to-all | bytes 786432 | tf_op jit(solution)/shard_map/all_to_all | solution.py:24
  117.1 0.1 broadcast_in_dim.43
  117.2 9.2 %all_to_all.45 = f32[2,256,384]{2,1,0:T(8,128)S(1)} all-to-all(f32[2,256,384]{2,1,0:T(8,128)S(1)} %broadcast_in_dim.43), channel_id=1, replica_groups=mesh['row'=12,'y'=8,'x'=4,'core'=2] {'core'}, dimensions={0} | all-to-all | bytes 1572864 | tf_op jit(solution)/shard_map/all_to_all | solution.py:24
  126.3 18.0 %shard_map.58.inverse_ref = f32[512,512]{1,0:T(8,128)S(1)} custom-call(f32[512,384]{1,0:T(8,128)S(1)} %bitcast.23), custom_call_target="tpu_custom_call" | custom-call | flops 1073741824 | bytes 67108864 | tf_op jit(solution)/shard_map/pallas_call | solution.py:172
  144.4 0.0 copy-start.3
  144.4 1.0 copy-done.3
  145.4 0.0 reduce-scatter.2.cloned.1.call-done
  145.4 0.0 copy-start.4
  145.4 23.4 %all_gather.3 = f32[480,512]{1,0:T(8,128)S(1)} all-gather(f32[40,512]{1,0:T(8,128)} %reduce-scatter.2.cloned.1.call-done), channel_id=1, replica_groups=mesh['row'=12,'y'=8,'x'=4,'core'=2] {'row'}, dimensions={0}, use_global_device_ids=true | all-gather | bytes 1064960 | tf_op jit(solution)/shard_map/all_gather | solution.py:226
  168.8 0.0 copy-done.4
  168.8 0.0 copy-start.7
  168.8 1.7 multiply_reduce_fusion
  170.4 0.7 broadcast_in_dim.44
  171.2 10.0 %all-to-all-start.7 = ((f32[64,1,512]{2,1,0:T(1,128)}), f32[64,1,512]{2,1,0:T(1,128)S(1)}, u32[]{:S(2)}, u32[]{:S(2)}) async-start(f32[64,1,512]{2,1,0:T(1,128)} %broadcast_in_dim.44), calls=%async_computation.8 | async-start | bytes 262144 | tf_op jit(solution)/shard_map/all_to_all | solution.py:24
  181.1 0.0 copy-done.7
  181.1 0.0 copy-start.5
  181.1 1.2 copy-done.5
  182.4 0.0 copy-start.6
  182.4 1.2 copy-done.6
  183.5 4.4 %shard_map.59 = (f32[512,512]{1,0:T(8,128)S(1)}, f32[448,512]{1,0:T(8,128)}) custom-call(f32[512,512]{1,0:T(8,128)S(1)} %bitcast.21, f32[512,512]{1,0:T(8,128)S(1)} %copy-done.5, f32[448,512]{1,0:T(8,128)S(1)} %get-tuple-element.13.right_ref, f32[448,512]{1,0:T(8,128)S(1)} %bitcast.22, bf16[448,512]{1,0:T(8,128)(2,1)S(1)} %bitcast.24), custom_call_target="tpu_custom_call" | custom-call | flops 8589934592 | bytes 8388608 | tf_op jit(solution)/shard_map/pallas_call | solution.py:211
  187.9 0.0 copy-start.1
  187.9 1.0 copy-done.1
  188.9 3.4 %all-to-all-done.7 = f32[64,1,512]{2,1,0:T(1,128)S(1)} async-done(((f32[64,1,512]{2,1,0:T(1,128)}), f32[64,1,512]{2,1,0:T(1,128)S(1)}, u32[]{:S(2)}, u32[]{:S(2)}) %all-to-all-start.7) | async-done | bytes 131104 | tf_op jit(solution)/shard_map/all_to_all | solution.py:24
  192.2 0.0 copy-start.2
  192.2 0.1 reduce_sum.49
  192.4 0.1 broadcast_multiply_fusion
  192.5 0.0 copy-start.8
  192.5 1.1 copy-done.2
  193.6 1.7 fusion
  195.2 0.0 copy-done.8
  (8 shorter events, 0.1 us)
Async XLA Ops:
  7.2 1.6 copy-start
  46.0 20.5 %all-to-all-start.2 = ((f32[32,8,512]{2,1,0:T(8,128)}), f32[32,8,512]{2,1,0:T(8,128)S(1)}, u32[]{:S(2)}, u32[]{:S(2)}) async-start(f32[32,8,512]{2,1,0:T(8,128)} %broadcast_in_dim.16), calls=%async_computation.2 | async-start | bytes 1048576 | tf_op jit(solution)/shard_map/all_to_all | solution.py:24
  51.1 94.2 %reduce-scatter.2.cloned.1.call-start = ((), (), s32[]{:S(2)}) async-start(), calls=%async_computation.9 | async-start | bytes 1064960 | tf_op jit(solution)/shard_map/reduce_scatter | solution.py:225
  144.4 1.0 copy-start.3
  145.4 23.4 %copy-start.4 = (f32[512,512]{1,0:T(8,128)S(1)}, f32[512,512]{1,0:T(8,128)}, u32[]{:S(2)}) copy-start(f32[512,512]{1,0:T(8,128)} %copy-done.3) | copy-start | bytes 3145732
  168.8 12.4 %copy-start.7 = (bf16[512,448]{0,1:T(8,128)(2,1)S(1)}, bf16[512,448]{0,1:T(8,128)(2,1)}, u32[]{:S(2)}) copy-start(bf16[512,448]{0,1:T(8,128)(2,1)} %param.4) | copy-start | bytes 1376260
  171.2 21.1 %all-to-all-start.7 = ((f32[64,1,512]{2,1,0:T(1,128)}), f32[64,1,512]{2,1,0:T(1,128)S(1)}, u32[]{:S(2)}, u32[]{:S(2)}) async-start(f32[64,1,512]{2,1,0:T(1,128)} %broadcast_in_dim.44), calls=%async_computation.8 | async-start | bytes 262144 | tf_op jit(solution)/shard_map/all_to_all | solution.py:24
  181.1 1.2 copy-start.5
  182.4 1.2 copy-start.6
  187.9 1.0 copy-start.1
  192.2 1.3 copy-start.2
  192.5 2.7 %copy-start.8 = (f32[448,512]{1,0:T(8,128)}, f32[448,512]{1,0:T(8,128)S(1)}, u32[]{:S(2)}) copy-start(f32[448,512]{1,0:T(8,128)S(1)} %broadcast_multiply_fusion) | copy-start | bytes 2752516
Sparse Core Ops, SparseCore 0:
  77.2 50.2 reduce-scatter.1

commit v3 on v2

--- a/solution.py
+++ b/solution.py
@@ -203,7 +203,7 @@
     ortho = dot(inverse_ref[...], left_ref[...], (1, 0))
     ortho_ref[...] = ortho
     blend = momentum_ref[...] + gradient_ref[...].astype(jnp.float32)
-    next_ref[...] = blend - 0.05 * dot(right_ref[...], ortho, (1, 0))
+    next_ref[...] = blend - 0.05 * dot(right_ref[: next_ref.shape[0], :], ortho, (1, 0))
 
 
 def correct(left, inverse, right, momentum, gradient):
@@ -221,11 +221,6 @@
     )(left, inverse, right, momentum, gradient)
 
 
-def sum_rows(block):
-    share = lax.psum_scatter(block, "row", scatter_dimension=0, tiled=True)
-    return lax.all_gather(share, "row", axis=0, tiled=True)
-
-
 def shards(momentum, gradient, right_factor):
     rank = right_factor.shape[1]
     col = CHIPS + ("core",)
@@ -235,13 +230,15 @@
     piece = jnp.sum(spread(pack_strip(left, position)[None], "row"), axis=0)
     columns = blend.shape[1]
     spare = -columns % (TILE * lax.axis_size("row"))
-    crossed = sum_rows(dot(jnp.pad(blend, ((0, 0), (0, spare))), left, (0, 1)))[:columns]
+    crossed = dot(jnp.pad(blend, ((0, 0), (0, spare))), left, (0, 1))
+    share = lax.psum_scatter(crossed, "row", scatter_dimension=0, tiled=True)
     inverse = inverse_factor(gather_columns(piece))
-    right = dot(crossed, inverse, (1, 1))
-    squares = jnp.sum(spread(jnp.sum(right * right, axis=0)[None], col), axis=0)
-    total_cols = right.shape[0] * lax.axis_size(col)
+    right = lax.all_gather(dot(share, inverse, (1, 1)), "row", axis=0, tiled=True)
+    squares = jnp.sum(right * right, axis=0).reshape(1, -1, LANES)
+    squares = jnp.sum(spread(squares, col), axis=0).reshape(rank)
+    total_cols = columns * lax.axis_size(col)
     total_rows = blend.shape[0] * lax.axis_size("row")
-    right_next = right * lax.rsqrt(squares / total_cols + 1e-06)
+    right_next = right[:columns] * lax.rsqrt(squares / total_cols + 1e-06)
     ortho, momentum_next = correct(left, inverse, right, momentum.T, gradient.T)
     factor = jnp.sqrt(jnp.float32(total_rows) / rank)
     update = (factor * dot(right_next, ortho, (1, 0), HIGH)).astype(jnp.bfloat16)

time: 203 us -> 203 us (level)
    unnamed x18 -> x16, local copies, waits for them, and re-layouts: 5.47 us -> 5.63 us
where the time goes in v3:
time: 203 us; the launch traced here: 202 us
  blocking collectives  113 us (56%)
  Pallas kernels  22.4 us (11%)
  waiting for transfers between devices  18.7 us (9%)
  starting transfers between devices  15 us (7%)
  between operations  14.2 us (7%)
  matrix products  9.18 us (5%)
  local copies, waits for them, and re-layouts  7.38 us (4%)
    all_to_all x6, blocking collectives, exchange(): return lax.all_to_all(blocks, axis, 0, 0, tiled=True)  90.1 us
    all_gather x1, blocking collectives, shards(): lax.all_gather(dot(share, inverse, (1, 1)), 'row', axis=0, tiled=True)  23 us
    all_to_all x2, waiting for transfers between devices, exchange(): return lax.all_to_all(blocks, axis, 0, 0, tiled=True)  18.7 us
    pallas_call x1, Pallas kernels, inverse_factor(): pl.pallas_call(inverse_factor_kernel, out_shape=jax.ShapeDtypeStruct(squa...  18 us
    all_to_all x2, starting transfers between devices, exchange(): return lax.all_to_all(blocks, axis, 0, 0, tiled=True)  15 us
    dot_general x5, matrix products, dot(): lax.dot_general(a, b, ((dims[:1], dims[1:]), ((), ())), precision=precisi...  9.18 us
    unnamed x16, local copies, waits for them, and re-layouts  5.63 us
    pallas_call x1, Pallas kernels, correct(): pl.pallas_call(correct_kernel, out_shape=(jax.ShapeDtypeStruct(left.shape...  4.36 us
  transfers between devices with their start and end apart: 3, of which 2 were waited for; matrix products, arithmetic and copies ran while one was open for 1% of the time, Pallas kernels for 11%

profile of v3, /device:TPU:1, one launch (start us, length us, event | category | flops | bytes accessed | tf_op | source)
XLA Modules:
  0.0 202.0 jit_solution(1145578327645330871)
XLA Ops:
  7.2 0.0 copy-start
  7.2 1.5 convert_add_fusion
  8.7 0.1 copy-done
  8.8 1.9 fusion.11
  10.7 14.7 %all_to_all.40 = f32[2,256,512]{2,1,0:T(8,128)S(1)} all-to-all(f32[2,256,512]{2,1,0:T(8,128)S(1)} %bitcast.29), channel_id=1, replica_groups=mesh['row'=12,'y'=8,'x'=4,'core'=2] {'core'}, dimensions={0} | all-to-all | bytes 2097152 | tf_op jit(solution)/shard_map/all_to_all | solution.py:24
  25.4 0.1 reduce_sum.45
  25.5 19.6 %all_to_all.41 = f32[32,8,512]{2,1,0:T(8,128)S(1)} all-to-all(f32[32,8,512]{2,1,0:T(8,128)S(1)} %bitcast.31), channel_id=1, replica_groups=mesh['row'=12,'y'=8,'x'=4,'core'=2] {'y','x'}, dimensions={0} | all-to-all | bytes 1048576 | tf_op jit(solution)/shard_map/all_to_all | solution.py:24
  45.2 0.9 broadcast_in_dim.18
  46.0 5.1 %all-to-all-start.2 = ((f32[32,8,512]{2,1,0:T(8,128)}), f32[32,8,512]{2,1,0:T(8,128)S(1)}, u32[]{:S(2)}, u32[]{:S(2)}) async-start(f32[32,8,512]{2,1,0:T(8,128)} %broadcast_in_dim.18), calls=%async_computation.2 | async-start | bytes 1048576 | tf_op jit(solution)/shard_map/all_to_all | solution.py:24
  51.1 0.0 reduce-scatter.2.cloned.1.call-start
  51.2 15.3 %all-to-all-done.2 = f32[32,8,512]{2,1,0:T(8,128)S(1)} async-done(((f32[32,8,512]{2,1,0:T(8,128)}), f32[32,8,512]{2,1,0:T(8,128)S(1)}, u32[]{:S(2)}, u32[]{:S(2)}) %all-to-all-start.2) | async-done | bytes 524320 | tf_op jit(solution)/shard_map/all_to_all | solution.py:24
  66.6 0.1 broadcast_in_dim.20
  66.7 7.6 %all_to_all.42 = f32[2,256,512]{2,1,0:T(8,128)S(1)} all-to-all(f32[2,256,512]{2,1,0:T(8,128)S(1)} %broadcast_in_dim.20), channel_id=1, replica_groups=mesh['row'=12,'y'=8,'x'=4,'core'=2] {'core'}, dimensions={0} | all-to-all | bytes 2097152 | tf_op jit(solution)/shard_map/all_to_all | solution.py:24
  74.3 2.7 %fusion.1 = f32[480,512]{1,0:T(8,128)} fusion(f32[512,512]{1,0:T(8,128)S(1)} %bitcast.22, f32[512,448]{0,1:T(8,128)S(1)} %convert_add_fusion), kind=kOutput, calls=%fused_computation.3 | convolution fusion | flops 1509949440 | bytes 2949120 | tf_op jit(solution)/shard_map/dot_general | solution.py:18
  77.0 0.0 reduce-scatter.2.cloned.1.call-update
  77.0 1.0 fusion.3
  78.0 23.5 %all_to_all.43 = f32[12,1,8,384]{3,2,1,0:T(8,128)S(1)} all-to-all(f32[12,1,8,384]{3,2,1,0:T(8,128)S(1)} %broadcast_in_dim.42), channel_id=1, replica_groups=mesh['row'=12,'y'=8,'x'=4,'core'=2] {'row'}, dimensions={0} | all-to-all | bytes 294912 | tf_op jit(solution)/shard_map/all_to_all | solution.py:24
  101.6 15.4 %all_to_all.44 = f32[32,8,384]{2,1,0:T(8,128)S(1)} all-to-all(f32[32,8,384]{2,1,0:T(8,128)S(1)} %broadcast_in_dim.43), channel_id=1, replica_groups=mesh['row'=12,'y'=8,'x'=4,'core'=2] {'y','x'}, dimensions={0} | all-to-all | bytes 786432 | tf_op jit(solution)/shard_map/all_to_all | solution.py:24
  117.0 0.1 broadcast_in_dim.45
  117.1 9.2 %all_to_all.45 = f32[2,256,384]{2,1,0:T(8,128)S(1)} all-to-all(f32[2,256,384]{2,1,0:T(8,128)S(1)} %broadcast_in_dim.45), channel_id=1, replica_groups=mesh['row'=12,'y'=8,'x'=4,'core'=2] {'core'}, dimensions={0} | all-to-all | bytes 1572864 | tf_op jit(solution)/shard_map/all_to_all | solution.py:24
  126.3 18.0 %shard_map.58.inverse_ref = f32[512,512]{1,0:T(8,128)S(1)} custom-call(f32[512,384]{1,0:T(8,128)S(1)} %bitcast.27), custom_call_target="tpu_custom_call" | custom-call | flops 1073741824 | bytes 67108864 | tf_op jit(solution)/shard_map/pallas_call | solution.py:172
  144.3 0.0 reduce-scatter.2.cloned.1.call-done
  144.4 2.0 fusion.12
  146.3 0.0 copy-start.3
  146.3 1.0 copy-done.3
  147.3 23.0 %all_gather.3.right_ref = f32[480,512]{1,0:T(8,128)S(1)} all-gather(f32[40,512]{1,0:T(8,128)S(1)} %fusion.12), channel_id=1, replica_groups=mesh['row'=12,'y'=8,'x'=4,'core'=2] {'row'}, dimensions={0}, use_global_device_ids=true | all-gather | bytes 1064960 | tf_op jit(solution)/shard_map/all_gather | solution.py:236
  170.3 0.0 copy-start.6
  170.3 0.1 multiply_reduce_fusion
  170.4 0.7 broadcast_in_dim.47
  171.1 9.9 %all-to-all-start.7 = ((f32[64,1,4,128]{3,2,1,0:T(4,128)}), f32[64,1,4,128]{3,2,1,0:T(4,128)S(1)}, u32[]{:S(2)}, u32[]{:S(2)}) async-start(f32[64,1,4,128]{3,2,1,0:T(4,128)} %broadcast_in_dim.47), calls=%async_computation.8 | async-start | bytes 262144 | tf_op jit(solution)/shard_map/all_to_all | solution.py:24
  181.0 0.0 copy-done.6
  181.0 0.0 copy-start.4
  181.0 1.2 copy-done.4
  182.2 0.0 copy-start.5
  182.2 1.2 copy-done.5
  183.4 4.4 %shard_map.59 = (f32[512,512]{1,0:T(8,128)S(1)}, f32[448,512]{1,0:T(8,128)}) custom-call(f32[512,512]{1,0:T(8,128)S(1)} %bitcast.25, f32[512,512]{1,0:T(8,128)S(1)} %copy-done.4, f32[480,512]{1,0:T(8,128)S(1)} %all_gather.3.right_ref, f32[448,512]{1,0:T(8,128)S(1)} %bitcast.26, bf16[448,512]{1,0:T(8,128)(2,1)S(1)} %bitcast.28), custom_call_target="tpu_custom_call" | custom-call | flops 8589934592 | bytes 8388608 | tf_op jit(solution)/shard_map/pallas_call | solution.py:211
  187.8 0.0 copy-start.1
  187.8 1.0 copy-done.1
  188.8 3.4 %all-to-all-done.7 = f32[64,1,4,128]{3,2,1,0:T(4,128)S(1)} async-done(((f32[64,1,4,128]{3,2,1,0:T(4,128)}), f32[64,1,4,128]{3,2,1,0:T(4,128)S(1)}, u32[]{:S(2)}, u32[]{:S(2)}) %all-to-all-start.7) | async-done | bytes 131104 | tf_op jit(solution)/shard_map/all_to_all | solution.py:24
  192.1 0.0 copy-start.2
  192.1 0.1 reduce_sum.49
  192.2 0.1 slice_multiply_fusion
  192.3 0.0 copy-start.7
  192.3 1.2 copy-done.2
  193.5 1.7 fusion
  195.2 0.0 copy-done.7
  (8 shorter events, 0.1 us)
Async XLA Ops:
  7.2 1.6 copy-start
  46.0 20.5 %all-to-all-start.2 = ((f32[32,8,512]{2,1,0:T(8,128)}), f32[32,8,512]{2,1,0:T(8,128)S(1)}, u32[]{:S(2)}, u32[]{:S(2)}) async-start(f32[32,8,512]{2,1,0:T(8,128)} %broadcast_in_dim.18), calls=%async_computation.2 | async-start | bytes 1048576 | tf_op jit(solution)/shard_map/all_to_all | solution.py:24
  51.1 93.2 %reduce-scatter.2.cloned.1.call-start = ((), (), s32[]{:S(2)}) async-start(), calls=%async_computation.9 | async-start | bytes 1064960 | tf_op jit(solution)/shard_map/reduce_scatter | solution.py:234
  146.3 1.0 copy-start.3
  170.3 10.7 %copy-start.6 = (bf16[512,448]{0,1:T(8,128)(2,1)S(1)}, bf16[512,448]{0,1:T(8,128)(2,1)}, u32[]{:S(2)}) copy-start(bf16[512,448]{0,1:T(8,128)(2,1)} %param.4) | copy-start | bytes 1376260
  171.1 21.0 %all-to-all-start.7 = ((f32[64,1,4,128]{3,2,1,0:T(4,128)}), f32[64,1,4,128]{3,2,1,0:T(4,128)S(1)}, u32[]{:S(2)}, u32[]{:S(2)}) async-start(f32[64,1,4,128]{3,2,1,0:T(4,128)} %broadcast_in_dim.47), calls=%async_computation.8 | async-start | bytes 262144 | tf_op jit(solution)/shard_map/all_to_all | solution.py:24
  181.0 1.2 copy-start.4
  182.2 1.2 copy-start.5
  187.8 1.0 copy-start.1
  192.1 1.4 copy-start.2
  192.3 2.9 %copy-start.7 = (f32[448,512]{1,0:T(8,128)}, f32[448,512]{1,0:T(8,128)S(1)}, u32[]{:S(2)}) copy-start(f32[448,512]{1,0:T(8,128)S(1)} %slice_multiply_fusion) | copy-start | bytes 2752516
Sparse Core Ops, SparseCore 0:
  77.1 50.2 reduce-scatter.1
